TPU v7x, 512 devices: a whole 4x8x8 slice. The times are simulated.
512 devices in a mesh: samp: 32 (over z, x_hi, core), par: 16 (over x_lo, y).
Axes of the slice: x: 4 (x_hi: 2, x_lo: 2; x = x_hi * 2 + x_lo), y: 8, z: 8, core: 2. Of those that a mesh axis runs over, the one named last changes fastest.
Arguments:
- activations: bfloat16 [512, 2, 64, 256], P('samp'), may hold values from 0 to 2
- cotangents: bfloat16 [512, 2, 64, 256], P('samp', None, 'par'), may hold values from -0.029907227 to 0.099609375
- energies: float32 [512], P('samp'), may hold values from -3 to -1
Outputs:
- update: float32 [64, 1152], P('par')
- coeffs: float32 [512], P('samp')
All inputs are finite; a program needn't handle non-finite values.
Results may differ from a plain program's by a relative error of at most 0.0034.
Values may be sent and summed in bfloat16 or wider, within the bound.
A program may use at most 64 MiB of HBM per device.

v0:
```python
import math
import jax
import jax.numpy as jnp
from jax import lax
from jax.sharding import PartitionSpec as P

C = 64
SIDE = 16
LAYERS = 2
reg_shift = 0.1


def sample_grads(activations, cotangents):
    sample_count, layer_count, channels, site_count = activations.shape
    owned_out = cotangents.shape[2]
    field = cotangents.reshape(sample_count, layer_count, owned_out, SIDE, SIDE)
    shifted = [
        jnp.roll(field, (row_step - 1, col_step - 1), axis=(3, 4))
        for row_step in range(3)
        for col_step in range(3)
    ]
    stacked = jnp.stack(shifted, axis=3).reshape(
        sample_count, layer_count, owned_out * 9, site_count
    )
    grads = jnp.einsum("slkx,slix->slki", stacked, activations, preferred_element_type=jnp.float32)
    grads = grads.reshape(sample_count, layer_count, owned_out, 9, channels).transpose(
        0, 2, 1, 4, 3
    )
    return grads.reshape(sample_count, owned_out * layer_count * channels * 9)


def contract(left_rows, right_rows):
    return lax.dot_general(
        left_rows, right_rows, (((1,), (1,)), ((), ())), preferred_element_type=jnp.float32
    )


def solve_system(gram, dev_all, total):
    regular = gram + reg_shift * jnp.eye(total, dtype=jnp.float32)
    factor = jnp.linalg.cholesky(regular)
    forward = lax.linalg.triangular_solve(factor, dev_all[:, None], left_side=True, lower=True)
    return lax.linalg.triangular_solve(
        factor, forward, left_side=True, lower=True, transpose_a=True
    )[:, 0]


def local(activations, cotangents, energies):
    grads = sample_grads(activations, cotangents)
    local_count = grads.shape[0]
    members = lax.axis_size("samp")
    position = lax.axis_index("samp")
    total = members * local_count
    params_all = LAYERS * C * C * 9
    scale = -math.sqrt(params_all / total)
    col_sums, energy_sum = lax.psum((jnp.sum(grads, axis=0), jnp.sum(energies)), "samp")
    centered = ((grads - col_sums / total) * (1.0 / math.sqrt(params_all))).astype(jnp.bfloat16)
    deviation = energies - energy_sum / total
    partial_value = contract(centered, lax.all_gather(centered, "samp", axis=0, tiled=True))
    summed = lax.psum(partial_value, "par")
    gram, dev_column = (
        lax.all_gather(summed, "samp", axis=0, tiled=True),
        lax.all_gather(deviation[:, None], "samp", axis=0, tiled=True),
    )
    dev_all = dev_column[:, 0]
    coeffs = solve_system(gram, dev_all, total)
    local_coeffs = lax.dynamic_slice_in_dim(coeffs, position * local_count, local_count)
    term = jnp.dot(
        local_coeffs[None, :], centered.astype(jnp.float32), precision=lax.Precision.HIGHEST
    )[0]
    summed_term = lax.psum(term, "samp")
    update = scale * summed_term
    return (update.reshape(cotangents.shape[2], -1), local_coeffs)


def solution(mesh):
    return jax.shard_map(
        local,
        mesh=mesh,
        in_specs=(P("samp", None, None, None), P("samp", None, "par", None), P("samp")),
        out_specs=(P("par", None), P("samp")),
        check_vma=False,
    )
```

profile of v0, /device:TPU:8, one launch (start us, length us, event | category | flops | bytes accessed | tf_op | source)
XLA Modules:
  0.0 767.5 jit_solution(1295712559334834222)
XLA Ops:
  7.2 1.3 reshape.131
  9.5 1.0 fusion.74
  10.5 1.2 fusion.75
  11.7 1.2 fusion.72
  12.9 1.2 fusion.73
  15.0 2.5 fusion.15
  17.5 0.9 bitcast_dynamic-update-slice_fusion.2
  18.5 1.1 fusion.16
  19.6 0.6 pad_maximum_fusion.1
  20.2 0.9 fusion.20
  21.1 0.9 copy_dynamic-update-slice_fusion
  22.0 0.9 fusion.19
  22.8 1.1 fusion.17
  24.0 0.9 bitcast_dynamic-update-slice_fusion.1
  24.8 1.1 fusion.18
  25.9 6.1 reshape.132
  32.7 2.7 copy.66
  35.7 0.6 reduce_sum.22
  36.5 76.6 %psum.30 = f32[]{:T(128)} all-reduce(f32[]{:T(128)} %reduce_sum.22), channel_id=1, replica_groups=mesh['samp'=32,'par'=16] {'samp'}, use_global_device_ids=true, to_apply=%region_12.13 | all-reduce | flops 1 | bytes 8 | tf_op jit(solution)/shard_map/psum | solution.py:55
  113.1 1.3 dynamic-slice.4
  115.8 128.5 %all-reduce.2 = (f32[4608]{0:T(1024)S(1)}, f32[512]{0:T(512)S(1)}) all-reduce(f32[4608]{0:T(1024)S(1)} %reduce_sum.21, f32[512]{0:T(512)S(1)} %subtract_dynamic-update-slice_fusion), channel_id=1, replica_groups=mesh['samp'=32,'par'=16] {'samp'}, use_global_device_ids=true, to_apply=%region_1.2 | all-reduce | flops 5120 | bytes 40960 | tf_op jit(solution)/shard_map/psum | solution.py:55
  244.3 3.4 reshape.134
  247.6 0.7 multiply_convert_fusion.1
  248.4 88.7 %all-gather.4.cloned.1.call-done = bf16[512,4608]{1,0:T(8,128)(2,1)} async-done(((bf16[16,4608]{1,0:T(8,128)(2,1)}), bf16[512,4608]{1,0:T(8,128)(2,1)}) %all-gather.4.cloned.1.call-update) | async-done | bytes 4718608 | tf_op jit(solution)/shard_map/all_gather | solution.py:58
  337.2 3.7 fusion.76
  340.9 58.7 %psum.29 = f32[16,512]{1,0:T(8,128)} all-reduce(f32[16,512]{1,0:T(8,128)S(1)} %fusion.76), channel_id=1, replica_groups=mesh['samp'=32,'par'=16] {'par'}, use_global_device_ids=true, to_apply=%region_2.3 | all-reduce | flops 8192 | bytes 65536 | tf_op jit(solution)/shard_map/psum | solution.py:59
  400.1 1.1 copy.79
  401.2 2.8 convert_element_type.12
  404.1 75.9 %all-gather.6.cloned.1.call-done = f32[512,512]{1,0:T(8,128)} async-done(((f32[16,512]{1,0:T(8,128)}), f32[512,512]{1,0:T(8,128)}) %all-gather.6.cloned.1.call-update) | async-done | bytes 1048592 | tf_op jit(solution)/shard_map/all_gather | solution.py:61
  480.0 1.6 copy.68
  481.5 1.1 select_add_fusion
  482.6 1.6 copy.69
  484.4 1.0 copy-done.1
  485.4 11.7 %cholesky.103 = f32[128,128]{1,0:T(8,128)S(1)} custom-call(f32[128,128]{1,0:T(8,128)S(1)} %cholesky.263), custom_call_target="Cholesky" | custom-call | tf_op jit(solution)/shard_map/jit(cholesky)/cholesky | solution.py:40
  497.2 9.8 %custom-call.32 = f32[1,128,128]{1,2,0:T(8,128)S(1)} custom-call(f32[1,128,128]{2,1,0:T(8,128)S(1)} %get-tuple-element.55), custom_call_target="InvertDiagBlocksLowerTriangular" | custom-call | tf_op jit(solution)/shard_map/jit(cholesky)/cholesky | solution.py:40
  507.0 1.2 fusion.25
  508.2 1.3 convolution_subtract_fusion
  509.5 11.7 %cholesky.215 = f32[128,128]{1,0:T(8,128)S(1)} custom-call(f32[128,128]{1,0:T(8,128)S(1)} %cholesky.267), custom_call_target="Cholesky" | custom-call | tf_op jit(solution)/shard_map/jit(cholesky)/cholesky | solution.py:40
  521.7 10.0 %custom-call.33 = f32[1,128,128]{1,2,0:T(8,128)S(1)} custom-call(f32[1,128,128]{2,1,0:T(8,128)S(1)} %get-tuple-element.53), custom_call_target="InvertDiagBlocksLowerTriangular" | custom-call | tf_op jit(solution)/shard_map/jit(cholesky)/cholesky | solution.py:40
  532.1 1.5 convolution_subtract_fusion.1
  533.6 11.7 %cholesky.236 = f32[128,128]{1,0:T(8,128)S(1)} custom-call(f32[128,128]{1,0:T(8,128)S(1)} %cholesky.272), custom_call_target="Cholesky" | custom-call | tf_op jit(solution)/shard_map/jit(cholesky)/cholesky | solution.py:40
  545.4 9.8 %custom-call.34 = f32[1,128,128]{1,2,0:T(8,128)S(1)} custom-call(f32[1,128,128]{2,1,0:T(8,128)S(1)} %get-tuple-element.51), custom_call_target="InvertDiagBlocksLowerTriangular" | custom-call | tf_op jit(solution)/shard_map/jit(cholesky)/cholesky | solution.py:40
  555.6 1.3 convolution_subtract_fusion.2
  556.9 12.0 %cholesky.253 = f32[128,128]{1,0:T(8,128)S(1)} custom-call(f32[128,128]{1,0:T(8,128)S(1)} %convolution_subtract_fusion.2), custom_call_target="Cholesky" | custom-call | tf_op jit(solution)/shard_map/jit(cholesky)/cholesky | solution.py:40
  569.0 0.7 compare_reduce_fusion.2
  569.7 0.6 compare_reduce_fusion.3
  570.3 0.6 compare_reduce_fusion.1
  571.0 0.7 compare_reduce_fusion
  574.3 11.3 %while.1 = (s32[]{:T(128)}, f32[512,512]{0,1:T(8,128)S(1)}, s32[4,2]{0,1:T(2,128)S(1)}, f32[4,128,128]{2,1,0:T(8,128)}, s32[]{:T(128)}) while((s32[]{:T(128)}, f32[512,512]{0,1:T(8,128)S(1)}, s32[4,2]{0,1:T(2,128)S(1)}, f32[4,128,128]{2,1,0:T(8,128)}, s32[]{:T(128)}) %tuple.39), condition=%wide.while_cond, body=%wide.while_body.sunk | while | flops 2 | bytes 393829 | solution.py:42
  574.4 0.6 fusion.100
  575.0 1.4 dynamic-slice.9
  576.5 0.6 bitcast_dynamic-update-slice_fusion.4
  577.2 0.6 fusion.100
  577.8 1.4 dynamic-slice.9
  579.4 0.6 bitcast_dynamic-update-slice_fusion.4
  580.0 0.6 fusion.100
  580.6 1.4 dynamic-slice.9
  582.2 0.6 bitcast_dynamic-update-slice_fusion.4
  582.9 0.6 fusion.100
  583.5 1.4 dynamic-slice.9
  585.0 0.6 bitcast_dynamic-update-slice_fusion.4
  585.6 40.1 %custom-call.35 = f32[4,128,128]{1,2,0:T(8,128)S(1)} custom-call(f32[4,128,128]{2,1,0:T(8,128)} %get-tuple-element.9), custom_call_target="InvertDiagBlocksLowerTriangular" | custom-call | tf_op jit(solution)/shard_map/triangular_solve | solution.py:42
  629.0 130.5 %psum.31 = f32[4608]{0:T(1024)S(1)} all-reduce(f32[4608]{0:T(1024)S(1)} %convolution_reduce_fusion), channel_id=1, replica_groups=mesh['samp'=32,'par'=16] {'samp'}, use_global_device_ids=true, to_apply=%region_13.14 | all-reduce | flops 4608 | bytes 36864 | tf_op jit(solution)/shard_map/psum | solution.py:70
  759.6 0.6 reshape.144
  (89 shorter events, 9.3 us)
Async XLA Ops:
  7.2 24.9 %copy-start = (bf16[16,2,64,256]{3,2,1,0:T(8,128)(2,1)S(1)}, bf16[16,2,64,256]{3,2,1,0:T(8,128)(2,1)}, u32[]{:S(2)}) copy-start(bf16[16,2,64,256]{3,2,1,0:T(8,128)(2,1)} %param.3) | copy-start | bytes 3145732
  7.2 330.0 %all-gather.4.cloned.1.call-start = ((), (), s32[]{:S(2)}) async-start(), calls=%async_computation | async-start | bytes 4866048 | tf_op jit(solution)/shard_map/all_gather | solution.py:58
  9.5 4.6 copy-start.7
  14.5 4.0 copy-start.2
  14.5 5.1 copy-start.3
  14.5 5.1 copy-start.4
  14.5 5.1 copy-start.5
  14.5 5.1 copy-start.6
  32.0 3.7 copy-start.9
  248.4 231.6 %all-gather.6.cloned.1.call-start = ((), (), s32[]{:S(2)}) async-start(), calls=%async_computation.1 | async-start | bytes 1081344 | tf_op jit(solution)/shard_map/all_gather | solution.py:61
  484.4 1.0 copy-start.1
  628.8 131.4 %copy-start.8 = (f32[16,1]{0,1:T(1,128)}, f32[16,1]{0,1:T(1,128)S(1)}, u32[]{:S(2)}) copy-start(f32[16,1]{0,1:T(1,128)S(1)} %fusion.59) | copy-start | bytes 196
Sparse Core Ops, SparseCore 0:
  248.5 88.6 all-gather.3
  399.8 80.1 all-gather.5
where the time goes:
time: 777 us; the launch traced here: 767 us
  blocking collectives  394 us (51%)
  waiting for transfers between devices  165 us (21%)
  other arithmetic  130 us (17%)
  local copies, waits for them, and re-layouts  46.6 us (6%)
  between operations  18.8 us (2%)
  matrix products  13.2 us (2%)
    psum x2, blocking collectives, local(): lax.psum((jnp.sum(grads, axis=0), jnp.sum(energies)), 'samp')  205 us
    psum x1, blocking collectives, local(): summed_term = lax.psum(term, 'samp')  131 us
    all_gather x1, waiting for transfers between devices, local(): lax.all_gather(centered, 'samp', axis=0, tiled=True)  88.7 us
    another operation x15, other arithmetic, solve_system(): factor = jnp.linalg.cholesky(regular)  79.5 us
    all_gather x1, waiting for transfers between devices, local(): lax.all_gather(summed, 'samp', axis=0, tiled=True)  75.9 us
    psum x1, blocking collectives, local(): summed = lax.psum(partial_value, 'par')  58.7 us
    another operation x4, other arithmetic, solve_system(): lax.linalg.triangular_solve(factor, forward, left_side=True, lower=True,...  40.4 us
  transfers between devices with their start and end apart: 2, of which 2 were waited for; matrix products, arithmetic and copies ran while one was open for 1% of the time, Pallas kernels for 0%

commit v1 on v0

--- a/solution.py
+++ b/solution.py
@@ -8,6 +8,7 @@
 SIDE = 16
 LAYERS = 2
 reg_shift = 0.1
+create_local_data = lambda my_tile: jnp.sum(lax.all_gather(my_tile, "par"), axis=0)
 
 
 def sample_grads(activations, cotangents):
@@ -56,7 +57,7 @@
     centered = ((grads - col_sums / total) * (1.0 / math.sqrt(params_all))).astype(jnp.bfloat16)
     deviation = energies - energy_sum / total
     partial_value = contract(centered, lax.all_gather(centered, "samp", axis=0, tiled=True))
-    summed = lax.psum(partial_value, "par")
+    summed = create_local_data(partial_value)
     gram, dev_column = (
         lax.all_gather(summed, "samp", axis=0, tiled=True),
         lax.all_gather(deviation[:, None], "samp", axis=0, tiled=True),

time: 777 us -> 750 us (0.965)
  blocking collectives: 394 us -> 369 us
    psum x1 -> x0, blocking collectives: 58.7 us -> none  [local(): summed = lax.psum(partial_value, 'par')]
    all_gather x0 -> x1, blocking collectives: none -> 33 us  [lax.all_gather(my_tile, 'par')]
where the time goes in v1:
time: 750 us; the launch traced here: 740 us
  blocking collectives  369 us (49%)
  waiting for transfers between devices  163 us (22%)
  other arithmetic  130 us (17%)
  local copies, waits for them, and re-layouts  46.6 us (6%)
  between operations  18.8 us (3%)
  matrix products  13.2 us (2%)
    psum x2, blocking collectives, local(): lax.psum((jnp.sum(grads, axis=0), jnp.sum(energies)), 'samp')  205 us
    psum x1, blocking collectives, local(): summed_term = lax.psum(term, 'samp')  131 us
    all_gather x1, waiting for transfers between devices, local(): lax.all_gather(centered, 'samp', axis=0, tiled=True)  88.7 us
    another operation x15, other arithmetic, solve_system(): factor = jnp.linalg.cholesky(regular)  79.5 us
    all_gather x1, waiting for transfers between devices, local(): lax.all_gather(summed, 'samp', axis=0, tiled=True)  74 us
    another operation x4, other arithmetic, solve_system(): lax.linalg.triangular_solve(factor, forward, left_side=True, lower=True,...  40.4 us
    all_gather x1, blocking collectives, lax.all_gather(my_tile, 'par')  33 us
  transfers between devices with their start and end apart: 2, of which 2 were waited for; matrix products, arithmetic and copies ran while one was open for 1% of the time, Pallas kernels for 0%

profile of v1, /device:TPU:8, one launch (start us, length us, event | category | flops | bytes accessed | tf_op | source)
XLA Modules:
  0.0 740.5 jit_solution(8483731953948945525)
XLA Ops:
  7.2 1.3 reshape.131
  9.5 1.0 fusion.74
  10.5 1.2 fusion.75
  11.7 1.2 fusion.72
  12.9 1.2 fusion.73
  15.0 2.5 fusion.15
  17.5 0.9 bitcast_dynamic-update-slice_fusion.2
  18.5 1.1 fusion.16
  20.2 0.9 fusion.20
  21.1 0.9 copy_dynamic-update-slice_fusion
  22.0 0.9 fusion.19
  22.8 1.1 fusion.17
  24.0 0.9 bitcast_dynamic-update-slice_fusion.1
  24.8 1.1 fusion.18
  25.9 6.1 reshape.132
  32.7 2.7 copy.64
  35.7 0.6 reduce_sum.32
  36.5 76.6 %psum.22 = f32[]{:T(128)} all-reduce(f32[]{:T(128)} %reduce_sum.32), channel_id=1, replica_groups=mesh['samp'=32,'par'=16] {'samp'}, use_global_device_ids=true, to_apply=%region_12.13 | all-reduce | flops 1 | bytes 8 | tf_op jit(solution)/shard_map/psum | solution.py:56
  113.1 1.3 dynamic-slice.4
  115.8 128.5 %all-reduce.2 = (f32[4608]{0:T(1024)S(1)}, f32[512]{0:T(512)S(1)}) all-reduce(f32[4608]{0:T(1024)S(1)} %reduce_sum.30, f32[512]{0:T(512)S(1)} %subtract_dynamic-update-slice_fusion), channel_id=1, replica_groups=mesh['samp'=32,'par'=16] {'samp'}, use_global_device_ids=true, to_apply=%region_1.2 | all-reduce | flops 5120 | bytes 40960 | tf_op jit(solution)/shard_map/psum | solution.py:56
  244.3 3.4 reshape.134
  247.6 0.7 multiply_convert_fusion.1
  248.4 88.7 %all-gather.5.cloned.1.call-done = bf16[512,4608]{1,0:T(8,128)(2,1)} async-done(((bf16[16,4608]{1,0:T(8,128)(2,1)}), bf16[512,4608]{1,0:T(8,128)(2,1)}) %all-gather.5.cloned.1.call-update) | async-done | bytes 4718608 | tf_op jit(solution)/shard_map/all_gather | solution.py:59
  337.2 3.7 fusion.76
  340.9 33.0 %all-gather = f32[256,512]{1,0:T(8,128)S(1)} all-gather(f32[16,512]{1,0:T(8,128)S(1)} %fusion.76), channel_id=2, replica_groups=mesh['samp'=32,'par'=16] {'par'}, dimensions={0}, use_global_device_ids=true | all-gather | bytes 557056 | tf_op jit(solution)/shard_map/all_gather | solution.py:11
  373.9 0.6 reduce_sum.31
  375.0 1.1 copy.77
  376.1 2.8 convert_element_type.12
  379.0 74.0 %all-gather.7.cloned.1.call-done = f32[512,512]{1,0:T(8,128)} async-done(((f32[16,512]{1,0:T(8,128)}), f32[512,512]{1,0:T(8,128)}) %all-gather.7.cloned.1.call-update) | async-done | bytes 1048592 | tf_op jit(solution)/shard_map/all_gather | solution.py:62
  452.9 1.6 copy.66
  454.5 1.1 select_add_fusion
  455.6 1.6 copy.67
  457.4 1.0 copy-done.1
  458.4 11.7 %cholesky.103 = f32[128,128]{1,0:T(8,128)S(1)} custom-call(f32[128,128]{1,0:T(8,128)S(1)} %cholesky.263), custom_call_target="Cholesky" | custom-call | tf_op jit(solution)/shard_map/jit(cholesky)/cholesky | solution.py:41
  470.1 9.8 %custom-call.32 = f32[1,128,128]{1,2,0:T(8,128)S(1)} custom-call(f32[1,128,128]{2,1,0:T(8,128)S(1)} %get-tuple-element.55), custom_call_target="InvertDiagBlocksLowerTriangular" | custom-call | tf_op jit(solution)/shard_map/jit(cholesky)/cholesky | solution.py:41
  480.0 1.2 fusion.25
  481.2 1.3 convolution_subtract_fusion
  482.5 11.7 %cholesky.215 = f32[128,128]{1,0:T(8,128)S(1)} custom-call(f32[128,128]{1,0:T(8,128)S(1)} %cholesky.267), custom_call_target="Cholesky" | custom-call | tf_op jit(solution)/shard_map/jit(cholesky)/cholesky | solution.py:41
  494.7 10.0 %custom-call.33 = f32[1,128,128]{1,2,0:T(8,128)S(1)} custom-call(f32[1,128,128]{2,1,0:T(8,128)S(1)} %get-tuple-element.53), custom_call_target="InvertDiagBlocksLowerTriangular" | custom-call | tf_op jit(solution)/shard_map/jit(cholesky)/cholesky | solution.py:41
  505.0 1.5 convolution_subtract_fusion.1
  506.6 11.7 %cholesky.236 = f32[128,128]{1,0:T(8,128)S(1)} custom-call(f32[128,128]{1,0:T(8,128)S(1)} %cholesky.272), custom_call_target="Cholesky" | custom-call | tf_op jit(solution)/shard_map/jit(cholesky)/cholesky | solution.py:41
  518.4 9.8 %custom-call.34 = f32[1,128,128]{1,2,0:T(8,128)S(1)} custom-call(f32[1,128,128]{2,1,0:T(8,128)S(1)} %get-tuple-element.51), custom_call_target="InvertDiagBlocksLowerTriangular" | custom-call | tf_op jit(solution)/shard_map/jit(cholesky)/cholesky | solution.py:41
  528.5 1.3 convolution_subtract_fusion.2
  529.9 12.0 %cholesky.253 = f32[128,128]{1,0:T(8,128)S(1)} custom-call(f32[128,128]{1,0:T(8,128)S(1)} %convolution_subtract_fusion.2), custom_call_target="Cholesky" | custom-call | tf_op jit(solution)/shard_map/jit(cholesky)/cholesky | solution.py:41
  542.0 0.7 compare_reduce_fusion.2
  542.7 0.6 compare_reduce_fusion.3
  543.3 0.6 compare_reduce_fusion.1
  543.9 0.7 compare_reduce_fusion
  547.3 11.3 %while.1 = (s32[]{:T(128)}, f32[512,512]{0,1:T(8,128)S(1)}, s32[4,2]{0,1:T(2,128)S(1)}, f32[4,128,128]{2,1,0:T(8,128)}, s32[]{:T(128)}) while((s32[]{:T(128)}, f32[512,512]{0,1:T(8,128)S(1)}, s32[4,2]{0,1:T(2,128)S(1)}, f32[4,128,128]{2,1,0:T(8,128)}, s32[]{:T(128)}) %tuple.39), condition=%wide.while_cond, body=%wide.while_body.sunk | while | flops 2 | bytes 393829 | solution.py:43
  547.4 0.6 fusion.100
  548.0 1.4 dynamic-slice.9
  549.5 0.6 bitcast_dynamic-update-slice_fusion.4
  550.2 0.6 fusion.100
  550.8 1.4 dynamic-slice.9
  552.3 0.6 bitcast_dynamic-update-slice_fusion.4
  553.0 0.6 fusion.100
  553.6 1.4 dynamic-slice.9
  555.1 0.6 bitcast_dynamic-update-slice_fusion.4
  555.8 0.6 fusion.100
  556.4 1.4 dynamic-slice.9
  558.0 0.6 bitcast_dynamic-update-slice_fusion.4
  558.6 40.1 %custom-call.35 = f32[4,128,128]{1,2,0:T(8,128)S(1)} custom-call(f32[4,128,128]{2,1,0:T(8,128)} %get-tuple-element.9), custom_call_target="InvertDiagBlocksLowerTriangular" | custom-call | tf_op jit(solution)/shard_map/triangular_solve | solution.py:43
  602.0 130.5 %psum.23 = f32[4608]{0:T(1024)S(1)} all-reduce(f32[4608]{0:T(1024)S(1)} %convolution_reduce_fusion), channel_id=1, replica_groups=mesh['samp'=32,'par'=16] {'samp'}, use_global_device_ids=true, to_apply=%region_13.14 | all-reduce | flops 4608 | bytes 36864 | tf_op jit(solution)/shard_map/psum | solution.py:71
  732.6 0.6 reshape.144
  (90 shorter events, 9.8 us)
Async XLA Ops:
  7.2 24.9 %copy-start = (bf16[16,2,64,256]{3,2,1,0:T(8,128)(2,1)S(1)}, bf16[16,2,64,256]{3,2,1,0:T(8,128)(2,1)}, u32[]{:S(2)}) copy-start(bf16[16,2,64,256]{3,2,1,0:T(8,128)(2,1)} %param.3) | copy-start | bytes 3145732
  7.2 330.0 %all-gather.5.cloned.1.call-start = ((), (), s32[]{:S(2)}) async-start(), calls=%async_computation | async-start | bytes 4866048 | tf_op jit(solution)/shard_map/all_gather | solution.py:59
  9.5 4.6 copy-start.7
  14.5 4.0 copy-start.2
  14.5 5.1 copy-start.3
  14.5 5.1 copy-start.4
  14.5 5.1 copy-start.5
  14.5 5.1 copy-start.6
  32.0 3.7 copy-start.9
  248.4 204.6 %all-gather.7.cloned.1.call-start = ((), (), s32[]{:S(2)}) async-start(), calls=%async_computation.1 | async-start | bytes 1081344 | tf_op jit(solution)/shard_map/all_gather | solution.py:62
  457.4 1.0 copy-start.1
  601.8 131.4 %copy-start.8 = (f32[16,1]{0,1:T(1,128)}, f32[16,1]{0,1:T(1,128)S(1)}, u32[]{:S(2)}) copy-start(f32[16,1]{0,1:T(1,128)S(1)} %fusion.59) | copy-start | bytes 196
Sparse Core Ops, SparseCore 0:
  248.5 88.6 all-gather.4
  374.7 78.2 all-gather.6
